TPU v7x, 128 devices: a whole 4x4x4 slice. The times are simulated.
128 devices in a mesh: rng: 16 (over z_lo, x, core), az: 8 (over z_hi, y).
Axes of the slice: x: 4, y: 4, z: 4 (z_hi: 2, z_lo: 2; z = z_hi * 2 + z_lo), core: 2. Of those that a mesh axis runs over, the one named last changes fastest.
Arguments:
- residual: float32 [2, 2, 2048, 16384], P(None, None, 'az', 'rng'), may hold values from -45 to 45
- range_chirp: float32 [2, 256], replicated, may hold values from -0.25 to 0.25
- az_kernel: float32 [128, 2, 1024], P(('rng', 'az')), may hold values from -0.125 to 0.125
- image_now: float32 [2, 2, 2048, 16384], P(None, None, None, ('rng', 'az')), may hold values from -6 to 6
Outputs:
- image_next: float32 [2, 2, 2048, 16384], P(None, None, None, ('rng', 'az'))
- root_mean: float32 [], replicated
All inputs are finite; a program needn't handle non-finite values.
Results may differ from a plain program's by a relative error of at most 0.000051.
Values sent between devices are 32-bit elements; how exact they have to be, the bound alone decides.
A program may use at most 128 MiB of HBM per device.

v0:
```python
import jax
import jax.numpy as jnp
from jax import lax
from jax.sharding import PartitionSpec as P

step_size = 0.5
reg_weight = 0.25
epsilon = 1e-06


def padded_2(cells, sides, width):
    for axis, dim in sides:
        count = lax.axis_size(axis)
        ends = count - 1
        head = lax.slice_in_dim(cells, 0, width, axis=dim)
        tail = lax.slice_in_dim(cells, cells.shape[dim] - width, cells.shape[dim], axis=dim)
        cells = jnp.concatenate(
            [
                lax.ppermute(tail, axis, [(i, (i + 1) % count) for i in range(ends)]),
                cells,
                lax.ppermute(head, axis, [((i + 1) % count, i) for i in range(ends)]),
            ],
            axis=dim,
        )
    return cells


def toeplitz_rows(taps_vec, row_count, col_count):
    padded = jnp.concatenate(
        [taps_vec, jnp.zeros((col_count + 1 - taps_vec.shape[0],), taps_vec.dtype)]
    )
    flattened = jnp.tile(padded, row_count)[: row_count * col_count]
    return flattened.reshape(row_count, col_count)


def range_correlate(padded, range_chirp, tile_cols):
    tap_count = range_chirp.shape[1]
    span_cols = padded.shape[3] - tap_count
    tile_count = span_cols // tile_cols
    shifts = tap_count // tile_cols + 1
    length = tile_cols * shifts
    blocks = padded.reshape(padded.shape[0], 2, padded.shape[2], tile_count + shifts - 1, tile_cols)
    windows = jnp.concatenate(
        [blocks[:, :, :, offset : offset + tile_count] for offset in range(shifts)], axis=4
    )
    real_part = toeplitz_rows(range_chirp[0], tile_cols, length).T
    imag_part = toeplitz_rows(range_chirp[1], tile_cols, length).T
    matrix = jnp.stack(
        [jnp.stack([real_part, -imag_part], 1), jnp.stack([imag_part, real_part], 1)], 0
    )
    result = jnp.einsum("pqatm,qmoj->poatj", windows, matrix, precision=lax.Precision.HIGHEST)
    return result.reshape(padded.shape[0], 2, padded.shape[2], span_cols)


def azimuth_correlate(turned, kernel_pair):
    tap_count = kernel_pair.shape[1]
    tile_rows = tap_count // 2
    tile_count = turned.shape[2] // tile_rows
    padded = jnp.pad(turned, ((0, 0), (0, 0), (tile_rows, tile_rows), (0, 0)))
    blocks = padded.reshape(turned.shape[0], 2, tile_count + 2, tile_rows, turned.shape[3])
    windows = jnp.concatenate(
        [blocks[:, :, offset : offset + tile_count] for offset in range(3)], axis=3
    )
    real_part = toeplitz_rows(kernel_pair[0], tile_rows, 3 * tile_rows)
    imag_part = toeplitz_rows(kernel_pair[1], tile_rows, 3 * tile_rows)
    matrix = jnp.stack(
        [jnp.stack([real_part, imag_part], 1), jnp.stack([-imag_part, real_part], 1)], 0
    )
    result = jnp.einsum("oiqm,pqtmw->potiw", matrix, windows, precision=lax.Precision.HIGHEST)
    return result.reshape(turned.shape)


def laplacian(image_now, range_padded):
    az_padded = jnp.pad(image_now, ((0, 0), (0, 0), (1, 1), (0, 0)))
    result = 4.0 * image_now - az_padded[:, :, 2:, :] - az_padded[:, :, :-2, :]
    return result - range_padded[:, :, :, 2:] - range_padded[:, :, :, :-2]


def corner_turn(echo_part):
    return lax.all_to_all(echo_part, "az", split_axis=3, concat_axis=2, tiled=True)


def local(residual, range_chirp, az_kernel, image_now):
    own_sum = jnp.sum(residual * residual)
    grand_total = lax.psum(own_sum, ("rng", "az"))
    entries = (
        2.0 * residual.shape[2] * lax.axis_size("az") * residual.shape[3] * lax.axis_size("rng")
    )
    root_mean = jnp.sqrt(grand_total / entries + epsilon)
    tap_count = range_chirp.shape[1]
    half_taps = tap_count // 2
    turned = corner_turn(residual)
    padded = padded_2(turned, ((("rng", "az"), 3),), half_taps)
    ranged = range_correlate(padded, range_chirp, min(tap_count, turned.shape[3]))
    adjoint = azimuth_correlate(ranged, az_kernel[0])
    rimmed = padded_2(image_now, ((("rng", "az"), 3),), 1)
    image_next = image_now - step_size * (
        adjoint / root_mean + reg_weight * laplacian(image_now, rimmed)
    )
    return (image_next, root_mean)


def solution(mesh):
    placed = (
        P(None, None, "az", "rng"),
        P(),
        P(("rng", "az"), None, None),
        P(None, None, None, ("rng", "az")),
    )
    return jax.shard_map(
        local,
        mesh=mesh,
        in_specs=placed,
        out_specs=(P(None, None, None, ("rng", "az")), P()),
        check_vma=False,
    )
```

profile of v0, /device:TPU:0, one launch (start us, length us, event | category | flops | bytes accessed | tf_op | source)
XLA Modules:
  0.0 345.5 jit_solution(15150743927880672170)
XLA Ops:
  0.6 7.2 %copy.19 = f32[2,2,256,1024]{2,1,0,3:T(2,128)} copy(f32[2,2,256,1024]{3,2,1,0:T(8,128)} %param.4) | data formatting | bytes 8388608 | tf_op args[0]
  7.8 59.1 %all_to_all.18 = f32[2,2,256,1024]{2,1,0,3:T(2,128)} all-to-all(f32[2,2,256,1024]{2,1,0,3:T(2,128)} %copy.19), channel_id=1, replica_groups=mesh['rng'=16,'az'=8] {'az'}, dimensions={3} | all-to-all | bytes 8388608 | tf_op jit(solution)/shard_map/all_to_all | solution.py:80
  66.9 7.2 %copy.20 = f32[2,2,256,8,128]{4,2,3,1,0:T(8,128)} copy(f32[2,2,256,8,128]{2,1,0,4,3:T(2,128)} %bitcast.77) | data formatting | bytes 8388608 | tf_op jit(solution)/shard_map/all_to_all | solution.py:80
  74.2 1.3 collective-permute-start.1
  75.4 6.5 %collective-permute-start = (f32[2,2,2048,128]{3,2,1,0:T(8,128)}, f32[2,2,2048,128]{3,2,1,0:T(8,128)}, u32[]{:S(2)}, u32[]{:S(2)}) collective-permute-start(f32[2,2,2048,128]{3,2,1,0:T(8,128)} %bitcast.79), channel_id=1, source_target_pairs={{0,1},{1,2},{2,3},{3,4},{4,5},{5,6},{6,7},{7,8},{8,9},{9,10},{10,1... | collective-permute-start | bytes 12582920 | tf_op jit(solution)/shard_map/ppermute | solution.py:19
  82.0 8.0 %fusion.26 = (f32[2,2,2048,1]{3,2,1,0:T(8,128)}, f32[2,2,2048,1]{3,2,1,0:T(8,128)}) fusion(f32[2,2,2048,128]{3,2,1,0:T(8,128)} %param.7), kind=kLoop, calls=%fused_computation.39 | loop fusion | bytes 131072 | tf_op jit(solution)/shard_map/slice | solution.py:15
  90.0 0.0 copy-start.4
  90.0 0.0 copy-start.3
  90.0 2.9 copy.39
  92.9 1.3 collective-permute-start.3
  94.2 2.8 copy.38
  97.0 1.3 collective-permute-start.2
  98.3 0.0 copy-done.4
  98.4 0.0 copy-done.3
  98.5 0.3 tile.19
  98.8 0.7 reshape.48
  99.6 0.3 tile.17
  99.9 0.7 reshape.47
  100.6 0.2 tile.42
  100.9 3.9 %tile.43 = f32[786944]{0:T(1024)} reshape(f32[512,1537]{1,0:T(8,128)S(1)} %tile.42) | data formatting | bytes 6295552 | tf_op jit(solution)/shard_map/tile | solution.py:32
  104.7 3.7 %slice.81 = f32[786432]{0:T(1024)} slice(f32[786944]{0:T(1024)} %tile.43), slice={[0:786432]} | slice | bytes 6291456 | tf_op jit(solution)/shard_map/slice | solution.py:32
  108.5 2.8 stack_reshape.8
  111.3 1.9 neg.14
  113.2 2.0 tile.40
  115.2 5.8 %tile.41 = f32[786944]{0:T(1024)} reshape(f32[512,1537]{1,0:T(8,128)} %tile.40) | data formatting | bytes 6295552 | tf_op jit(solution)/shard_map/tile | solution.py:32
  121.0 3.8 %slice.80 = f32[786432]{0:T(1024)} slice(f32[786944]{0:T(1024)} %tile.41), slice={[0:786432]} | slice | bytes 6291456 | tf_op jit(solution)/shard_map/slice | solution.py:32
  124.7 0.0 copy-start.1
  124.7 4.5 %stack_reshape.7 = f32[512,1,1536]{2,0,1:T(8,128)} reshape(f32[786432]{0:T(1024)} %slice.80) | data formatting | bytes 6291456 | tf_op jit(solution)/shard_map/stack;reshape | solution.py:67
  129.3 0.0 copy-done.1
  129.3 0.0 copy-start
  129.3 4.0 %multiply_reduce_fusion = f32[]{:T(128)} fusion(f32[2,2,256,1024]{3,2,1,0:T(8,128)} %param.4), kind=kLoop, calls=%fused_computation.27 | loop fusion | flops 2097151 | bytes 4194308 | tf_op jit(solution)/shard_map/reduce_sum | solution.py:84
  133.3 0.0 copy-done
  133.3 0.0 copy-start.2
  133.3 8.0 %maximum_bitcast_fusion.6 = (f32[1,512,2,1536]{3,1,2,0:T(8,128)}, f32[1,512,2,1536]{3,1,2,0:T(8,128)}) fusion(f32[512,1,1536]{2,0,1:T(8,128)S(1)} %stack_reshape.8, f32[512,1,1536]{2,0,1:T(8,128)} %stack_reshape.7, f32[512,1,1536]{2,0,1:T(8,128)S(1)} %copy-done), kind=kLoop, calls=%fused_computation.15 | loop fusion | flops 3145728 | bytes 22020096 | tf_op jit(solution)/shard_map/stack | solution.py:66
  141.4 0.0 copy-done.2
  141.4 0.1 maximum_bitcast_fusion.16
  141.4 86.8 %psum.7 = f32[]{:T(128)} all-reduce(f32[]{:T(128)} %multiply_reduce_fusion), channel_id=1, replica_groups=mesh['rng'=16,'az'=8] {'rng','az'}, use_global_device_ids=true, to_apply=%region_1.0 | all-reduce | flops 1 | bytes 8 | tf_op jit(solution)/shard_map/psum | solution.py:85
  228.9 0.0 collective-permute-done.2
  229.0 2.6 copy.27
  231.6 0.0 collective-permute-done.3
  231.6 2.6 copy.29
  234.2 0.0 collective-permute-done.1
  234.2 0.0 collective-permute-done
  234.2 14.9 %fusion.19 = f32[2,2,2048,128]{2,3,0,1:T(8,128)} fusion(f32[2,2,2048,1,128]{4,2,1,0,3:T(8,128)} %bitcast.19, f32[2,2,2048,1,128]{4,2,1,0,3:T(8,128)} %bitcast.80, f32[2,2,2048,1,128]{4,2,1,0,3:T(8,128)} %bitcast.16, f32[1,384,2,128]{1,3,0,2:T(8,128)S(1)} %get-tuple-element.10, f32[1,384,2,128]{1,3,0,2:T(8,128)S(1)} %get-tuple-element.9), kind=kOutput, calls=%fused_computation.28 | convolution fusion | flops 9670164480 | bytes 17563648 | tf_op jit(solution)/shard_map/pqatm,qmoj->poatj/dot_general | solution.py:51
  249.1 5.4 %copy.40 = f32[2,2,2048,128]{3,2,1,0:T(8,128)} copy(f32[2,2,2048,128]{2,3,0,1:T(8,128)} %fusion.19) | data formatting | bytes 8388608
  254.5 2.6 pad.12.clone
  257.1 5.0 %fusion.25 = (f32[2,2,4,512,128]{4,3,2,1,0:T(8,128)}, f32[2,2,4,512,128]{4,3,2,1,0:T(8,128)}, f32[2,2,4,512,128]{4,3,2,1,0:T(8,128)}) fusion(f32[2,2,6,512,128]{4,3,2,1,0:T(8,128)S(1)} %bitcast.76), kind=kLoop, calls=%fused_computation.38 | loop fusion | bytes 25165824 | tf_op jit(solution)/shard_map/slice | solution.py:62
  262.1 5.3 %copy.35 = f32[2,2,4,512,128]{3,4,1,2,0:T(8,128)} copy(f32[2,2,4,512,128]{4,3,2,1,0:T(8,128)} %get-tuple-element.2) | data formatting | bytes 8388608
  267.4 5.2 %copy.36 = f32[2,2,4,512,128]{3,4,1,2,0:T(8,128)} copy(f32[2,2,4,512,128]{4,3,2,1,0:T(8,128)} %get-tuple-element.3) | data formatting | bytes 8388608
  272.6 5.2 %copy.37 = f32[2,2,4,512,128]{3,4,1,2,0:T(8,128)} copy(f32[2,2,4,512,128]{4,3,2,1,0:T(8,128)} %get-tuple-element.4) | data formatting | bytes 8388608
  277.8 46.5 %fusion.18 = f32[2,2,4,512,128]{3,4,1,2,0:T(8,128)} fusion(f32[1,512,2,1536]{3,1,2,0:T(8,128)} %get-tuple-element.8, f32[1,512,2,1536]{3,1,2,0:T(8,128)} %get-tuple-element.7, f32[2,2,4,512,128]{3,4,1,2,0:T(8,128)} %copy.37, f32[2,2,4,512,128]{3,4,1,2,0:T(8,128)} %copy.36, f32[2,2,4,512,128]{3,4,1,2,0:T(8,128)} %copy.35, f32[]{:T(128)} %sqrt.3), kind=kOutput, calls=%fused_computation.26 | convolution fusion | flops 38665191424 | bytes 29360132 | tf_op jit(solution)/shard_map/oiqm,pqtmw->potiw/dot_general | solution.py:69
  324.4 5.2 %copy.25 = f32[2,2,4,512,128]{4,3,2,1,0:T(8,128)} copy(f32[2,2,4,512,128]{3,4,1,2,0:T(8,128)} %fusion.18) | data formatting | bytes 8388608 | tf_op jit(solution)/shard_map/div | solution.py:98
  329.6 14.7 %fusion.16 = f32[2,2,2048,128]{3,2,1,0:T(8,128)} fusion(f32[2,2,2048,128]{3,2,1,0:T(8,128)} %param.7, f32[2,2,2048,1]{3,2,1,0:T(8,128)} %copy.29, f32[2,2,2048,1]{3,2,1,0:T(8,128)} %copy.27, f32[2,2,4,512,128]{4,3,2,1,0:T(8,128)} %copy.25), kind=kLoop, calls=%fused_computation.22 | loop fusion | flops 11534336 | bytes 12648448 | tf_op jit(solution)/shard_map/sub | solution.py:97
  (11 shorter events, 0.1 us)
Async XLA Ops:
  74.2 160.1 %collective-permute-start.1 = (f32[2,2,2048,128]{3,2,1,0:T(8,128)}, f32[2,2,2048,128]{3,2,1,0:T(8,128)}, u32[]{:S(2)}, u32[]{:S(2)}) collective-permute-start(f32[2,2,2048,128]{3,2,1,0:T(8,128)} %bitcast.78), channel_id=1, source_target_pairs={{1,0},{2,1},{3,2},{4,3},{5,4},{6,5},{7,6},{8,7},{9,8},{10,9},{11,1... | collective-permute-start | bytes 12582920 | tf_op jit(solution)/shard_map/ppermute | solution.py:21
  75.4 158.8 %collective-permute-start = (f32[2,2,2048,128]{3,2,1,0:T(8,128)}, f32[2,2,2048,128]{3,2,1,0:T(8,128)}, u32[]{:S(2)}, u32[]{:S(2)}) collective-permute-start(f32[2,2,2048,128]{3,2,1,0:T(8,128)} %bitcast.79), channel_id=1, source_target_pairs={{0,1},{1,2},{2,3},{3,4},{4,5},{5,6},{6,7},{7,8},{8,9},{9,10},{10,1... | collective-permute-start | bytes 12582920 | tf_op jit(solution)/shard_map/ppermute | solution.py:19
  90.0 8.3 %copy-start.4 = (f32[2,256]{1,0:T(2,128)S(1)}, f32[2,256]{1,0:T(2,128)}, u32[]{:S(2)}) copy-start(f32[2,256]{1,0:T(2,128)} %param.5) | copy-start | bytes 6148
  90.0 8.4 %copy-start.3 = (f32[1,2,1024]{2,1,0:T(2,128)S(1)}, f32[1,2,1024]{2,1,0:T(2,128)}, u32[]{:S(2)}) copy-start(f32[1,2,1024]{2,1,0:T(2,128)} %param.6) | copy-start | bytes 24580
  92.9 138.7 %collective-permute-start.3 = (f32[2,2,2048,1]{2,1,3,0:T(2,128)S(1)}, f32[2,2,2048,1]{2,1,3,0:T(2,128)S(1)}, u32[]{:S(2)}, u32[]{:S(2)}) collective-permute-start(f32[2,2,2048,1]{2,1,3,0:T(2,128)S(1)} %copy.39), channel_id=1, source_target_pairs={{0,1},{1,2},{2,3},{3,4},{4,5},{5,6},{6,7},{7,8},{8,9},{9,10},{10,1... | collective-permute-start | bytes 98312 | tf_op jit(solution)/shard_map/ppermute | solution.py:19
  97.0 131.9 %collective-permute-start.2 = (f32[2,2,2048,1]{2,1,3,0:T(2,128)S(1)}, f32[2,2,2048,1]{2,1,3,0:T(2,128)S(1)}, u32[]{:S(2)}, u32[]{:S(2)}) collective-permute-start(f32[2,2,2048,1]{2,1,3,0:T(2,128)S(1)} %copy.38), channel_id=1, source_target_pairs={{1,0},{2,1},{3,2},{4,3},{5,4},{6,5},{7,6},{8,7},{9,8},{10,9},{11,1... | collective-permute-start | bytes 98312 | tf_op jit(solution)/shard_map/ppermute | solution.py:21
  124.7 4.5 %copy-start.1 = (f32[128,384]{1,0:T(8,128)S(1)}, f32[128,384]{1,0:T(8,128)}, u32[]{:S(2)}) copy-start(f32[128,384]{1,0:T(8,128)} %reshape.48) | copy-start | bytes 589828
  129.3 4.0 %copy-start = (f32[512,1,1536]{2,0,1:T(8,128)S(1)}, f32[512,1,1536]{2,0,1:T(8,128)}, u32[]{:S(2)}) copy-start(f32[512,1,1536]{2,0,1:T(8,128)} %neg.14) | copy-start | bytes 9437188
  133.3 8.1 %copy-start.2 = (f32[128,384]{1,0:T(8,128)S(1)}, f32[128,384]{1,0:T(8,128)}, u32[]{:S(2)}) copy-start(f32[128,384]{1,0:T(8,128)} %reshape.47) | copy-start | bytes 589828
where the time goes:
time: 348 us; the launch traced here: 345 us
  blocking collectives  146 us (42%)
  local copies, waits for them, and re-layouts  96.3 us (28%)
  matrix products  61.4 us (18%)
  other arithmetic  28.8 us (8%)
  starting transfers between devices  10.4 us (3%)
    psum x1, blocking collectives, local(): grand_total = lax.psum(own_sum, ('rng', 'az'))  86.8 us
    all_to_all x1, blocking collectives, corner_turn(): lax.all_to_all(echo_part, 'az', split_axis=3, concat_axis=2, tiled=True)  59.1 us
    dot_general x1, matrix products, azimuth_correlate(): jnp.einsum('oiqm,pqtmw->potiw', matrix, windows, precision=lax.Precision....  46.5 us
    unnamed x17, local copies, waits for them, and re-layouts  34 us
    dot_general x1, matrix products, range_correlate(): jnp.einsum('pqatm,qmoj->poatj', windows, matrix, precision=lax.Precision....  14.9 us
    sub x1, other arithmetic, local(): image_now - step_size * (adjoint / root_mean + reg_weight * laplacian(ima...  14.7 us
    another operation x8, local copies, waits for them, and re-layouts, toeplitz_rows(): flattened = jnp.tile(padded, row_count)[:row_count * col_count]  12.6 us
    another operation x1, other arithmetic, azimuth_correlate(): jnp.stack([jnp.stack([real_part, imag_part], 1), jnp.stack([-imag_part, r...  8.05 us
  transfers between devices with their start and end apart: 4, of which 0 were waited for; matrix products, arithmetic and copies ran while one was open for 18% of the time, Pallas kernels for 0%

commit v1 on v0

v1 whole, which is shorter than its diff:
```python
import jax
import jax.numpy as jnp
from jax import lax
from jax.experimental import pallas as pl
from jax.experimental.pallas import tpu as pltpu
from jax.sharding import PartitionSpec as P

step_size = 0.5
reg_weight = 0.25
epsilon = 1e-06

F32 = jnp.float32
BF16 = jnp.bfloat16
MESH = pl.DeviceIdType.MESH
GROUP = 8
OTHERS = GROUP - 1
TURN = ((0, 1), (1, 0), (2, 1), (3, 0), (1, 1), (2, 0), (3, 1))
STAGES = 7


def dot(a, b):
    return jnp.dot(a, b, preferred_element_type=F32)


def split(value):
    high = value.astype(BF16)
    return high, (value - high.astype(F32)).astype(BF16)


def toeplitz(row, rows):
    wide = jnp.broadcast_to(row, (rows, row.shape[1]))
    return pltpu.roll(wide, 0, 1, stride=1, stride_axis=0)


def kernel(
    res, chirp, azk, img,
    out, rm_out,
    xf, xh, xl, ch, cl, lh, ll, sb, rv, yh, yl, acc, im, base, pk, pc, sm,
    ld, hs, hr, ss, rs, es, er, cs, cr, os,
):
    rng, az = lax.axis_index("rng"), lax.axis_index("az")
    zh, y = az // 4, az % 4
    flat = rng * 8 + az
    to_az = [((zh + dz) % 2) * 4 + (y + dy) % 4 for dy, dz in TURN]
    from_az = [((zh + dz) % 2) * 4 + (y + 4 - dy) % 4 for dy, dz in TURN]
    rng_next, rng_prev = (rng + 1) % 16, (rng + 15) % 16
    col_next, col_prev = (flat + 1) % 128, (flat + 127) % 128

    def partner(stage):
        width = 2**stage
        other = flat + (1 - 2 * ((flat // width) % 2)) * width
        return (other // 8, other % 8)

    load_img = pltpu.make_async_copy(img, im.at[:, :, pl.ds(8, 2048)], ld.at[8])

    def load_block(b):
        return pltpu.make_async_copy(
            res.at[:, :, :, pl.ds(128 * b, 128)], xf.at[b + 1], ld.at[b]
        )

    for b in range(8):
        load_block(b).start()
    load_img.start()

    barrier = pltpu.get_barrier_semaphore()
    peers = [(rng, to_az[t]) for t in range(OTHERS)]
    peers += [(rng_next, az), (rng_prev, az)]
    peers += [(col_next // 8, col_next % 8), (col_prev // 8, col_prev % 8)]
    peers += [partner(stage) for stage in range(STAGES)]
    for peer in peers:
        pl.semaphore_signal(barrier, inc=1, device_id=peer, device_id_type=MESH)

    lanes = jnp.zeros((1, 128), F32)
    cr_t = toeplitz(jnp.concatenate([chirp[0:1, :], lanes], 1), 128).T
    ci_t = toeplitz(jnp.concatenate([chirp[1:2, :], lanes], 1), 128).T
    for rows, left, right in ((0, cr_t, -ci_t), (384, ci_t, cr_t)):
        for cols, part in ((0, left), (128, right)):
            high, low = split(part)
            ch[rows : rows + 384, cols : cols + 128] = high
            cl[rows : rows + 384, cols : cols + 128] = low

    pl.semaphore_wait(barrier, len(peers))

    to_next = pltpu.make_async_remote_copy(
        src_ref=res.at[:, :, :, pl.ds(896, 128)], dst_ref=xf.at[0],
        send_sem=hs.at[0], recv_sem=hr.at[0],
        device_id=(rng_next, az), device_id_type=MESH,
    )
    to_prev = pltpu.make_async_remote_copy(
        src_ref=res.at[:, :, :, pl.ds(0, 128)], dst_ref=xf.at[9],
        send_sem=hs.at[1], recv_sem=hr.at[1],
        device_id=(rng_prev, az), device_id_type=MESH,
    )

    @pl.when(rng < 15)
    def _():
        to_next.start()

    @pl.when(rng > 0)
    def _():
        to_prev.start()

    def split_block(b):
        for p in range(2):
            for c in range(2):
                high, low = split(xf[b, p, c])
                xh[b, c, p * 256 : (p + 1) * 256] = high
                xl[b, c, p * 256 : (p + 1) * 256] = low

    sm[0] = jnp.zeros((8, 128), F32)
    for b in range(8):
        load_block(b).wait()

    def first(b, carry):
        split_block(b)
        total = sm[0]
        for p in range(2):
            for c in range(2):
                v = xf[b, p, c]
                total += jnp.sum((v * v).reshape(32, 8, 128), axis=0)
        sm[0] = total
        return carry

    lax.fori_loop(1, 9, first, 0)

    def range_block(j, slot):
        high = jnp.concatenate([xh[j + q, c] for c in range(2) for q in range(3)], 1)
        low = jnp.concatenate([xl[j + q, c] for c in range(2) for q in range(3)], 1)
        result = dot(high, ch[...]) + dot(low, ch[...]) + dot(high, cl[...])
        for p in range(2):
            for c in range(2):
                sb[slot, c * 256 : (c + 1) * 256, p * 128 : (p + 1) * 128] = result[
                    p * 256 : (p + 1) * 256, c * 128 : (c + 1) * 128
                ]

    def turn_copy(t):
        dz, dy = 1 - t % 2, t - 3 * (t // 4)
        target = ((zh + dz) % 2) * 4 + (y + dy) % 4
        return target, pltpu.make_async_remote_copy(
            src_ref=sb.at[t], dst_ref=rv.at[t], send_sem=ss.at[t], recv_sem=rs.at[t],
            device_id=(rng, target), device_id_type=MESH,
        )

    def inner(j):
        return jnp.logical_and(j > 0, j < 7)

    def send_inner(t, carry):
        target, copy = turn_copy(t)

        @pl.when(inner(target))
        def _():
            range_block(target, t)
            copy.start()

        return carry

    lax.fori_loop(0, OTHERS, send_inner, 0)

    lanes = jnp.zeros((1, 256), F32)
    wr = toeplitz(jnp.concatenate([azk[0, 0:1, :], lanes], 1), 256)
    wi = toeplitz(jnp.concatenate([azk[0, 1:2, :], lanes], 1), 256)
    for e in range(5):
        part_r, part_i = wr[:, 256 * e : 256 * e + 256], wi[:, 256 * e : 256 * e + 256]
        for rows, left, right in ((0, part_r, part_i), (256, -part_i, part_r)):
            for cols, part in ((0, left), (256, right)):
                high, low = split(part)
                lh[e, rows : rows + 256, cols : cols + 256] = high
                ll[e, rows : rows + 256, cols : cols + 256] = low

    @pl.when(rng > 0)
    def _():
        to_next.wait_recv()

    @pl.when(rng == 0)
    def _():
        xf[0] = jnp.zeros_like(xf[0])

    @pl.when(rng < 15)
    def _():
        to_prev.wait_recv()

    @pl.when(rng == 15)
    def _():
        xf[9] = jnp.zeros_like(xf[9])

    split_block(0)
    split_block(9)

    def send_outer(t, carry):
        target, copy = turn_copy(t)

        @pl.when(jnp.logical_not(inner(target)))
        def _():
            range_block(target, t)
            copy.start()

        return carry

    lax.fori_loop(0, OTHERS, send_outer, 0)
    range_block(az, OTHERS)

    load_img.wait()
    for p in range(2):
        for c in range(2):
            im[p, c, 0:8] = jnp.zeros((8, 128), F32)
            im[p, c, 2056:2064] = jnp.zeros((8, 128), F32)

    def pack(k, carry):
        at = pl.multiple_of(128 * k, 128)
        for p in range(2):
            for c in range(2):
                turned = im[p, c, pl.ds(at + 8, 128), :].T
                row = 2 * p + c
                pk[row : row + 1, pl.ds(at, 128)] = turned[0:1]
                pk[row + 4 : row + 5, pl.ds(at, 128)] = turned[127:128]
        return carry

    lax.fori_loop(0, 16, pack, 0)

    def column_copy(side, target):
        return pltpu.make_async_remote_copy(
            src_ref=pk, dst_ref=pc.at[side], send_sem=cs.at[side], recv_sem=cr.at[side],
            device_id=(target // 8, target % 8), device_id_type=MESH,
        )

    cols = [column_copy(0, col_next), column_copy(1, col_prev)]
    for copy in cols:
        copy.start()

    acc[...] = jnp.zeros_like(acc)

    def azimuth(source, s):
        high, low = split(source)
        yh[...] = high
        yl[...] = low

        def tile(e, carry):
            i = s + 2 - e

            @pl.when(jnp.logical_and(i >= 0, i < 8))
            def _():
                acc[i] += dot(lh[e], yh[...]) + dot(lh[e], yl[...]) + dot(ll[e], yh[...])

            return carry

        lax.fori_loop(0, 5, tile, 0)

    def sum_copy(stage):
        return pltpu.make_async_remote_copy(
            src_ref=sm.at[2 * stage], dst_ref=sm.at[2 * stage + 1],
            send_sem=es.at[stage], recv_sem=er.at[stage],
            device_id=partner(stage), device_id_type=MESH,
        )

    def regularize():
        for copy in cols:
            copy.wait_recv()
        lane = lax.broadcasted_iota(jnp.int32, (128, 128), 1)
        has_prev = jnp.where(flat > 0, 1.0, 0.0)
        has_next = jnp.where(flat < 127, 1.0, 0.0)

        def rows(k, carry):
            at = pl.multiple_of(128 * k, 128)
            before = pc[0, :, pl.ds(at, 128)].T * has_prev
            after = pc[1, :, pl.ds(at, 128)].T * has_next
            for p in range(2):
                for c in range(2):
                    row = 2 * p + c
                    v = im[p, c, pl.ds(at, 144), :]
                    mid = v[8:136]
                    left = jnp.where(lane == 0, before[:, row + 4 : row + 5], pltpu.roll(mid, 1, 1))
                    right = jnp.where(lane == 127, after[:, row : row + 1], pltpu.roll(mid, 127, 1))
                    lap = 4.0 * mid - v[9:137] - v[7:135] - right - left
                    base[p, c, pl.ds(at, 128), :] = mid - (step_size * reg_weight) * lap
            return carry

        lax.fori_loop(0, 16, rows, 0)

    for n in range(8):
        if n < STAGES:
            sum_copy(n).start()
        if n == 0:
            azimuth(sb[OTHERS], az)
        else:
            turn_copy(n - 1)[1].wait_recv()
            azimuth(rv[n - 1], from_az[n - 1])
        if n < STAGES:
            sum_copy(n).wait()
            sm[2 * n + 2] = sm[2 * n] + sm[2 * n + 1]
        if n == 1:
            regularize()

    entries = 2.0 * 2048 * 16384
    total = jnp.sum(sm[2 * STAGES], axis=(0, 1), keepdims=True)
    root_mean = jnp.sqrt(total / entries + epsilon)
    rm_out[...] = root_mean
    scale = step_size / root_mean

    def out_copy(i):
        lines = pl.ds(pl.multiple_of(256 * i, 256), 256)
        return pltpu.make_async_copy(base.at[:, :, lines], out.at[:, :, lines], os.at[i])

    def finish(i, carry):
        at = pl.multiple_of(256 * i, 256)
        for p in range(2):
            for c in range(2):
                base[p, c, pl.ds(at, 256), :] = (
                    base[p, c, pl.ds(at, 256), :]
                    - acc[i, c * 256 : (c + 1) * 256, p * 128 : (p + 1) * 128] * scale
                )
        out_copy(i).start()
        return carry

    lax.fori_loop(0, 8, finish, 0)

    for i in range(8):
        out_copy(i).wait()
    for t in range(OTHERS):
        turn_copy(t)[1].wait_send()
    for copy in cols:
        copy.wait_send()

    @pl.when(rng < 15)
    def _():
        to_next.wait_send()

    @pl.when(rng > 0)
    def _():
        to_prev.wait_send()


def local(residual, range_chirp, az_kernel, image_now):
    vmem = pl.BlockSpec(memory_space=pltpu.VMEM)
    anywhere = pl.BlockSpec(memory_space=pl.ANY)
    dma = pltpu.SemaphoreType.DMA
    image_next, root_mean = pl.pallas_call(
        kernel,
        out_shape=(
            jax.ShapeDtypeStruct(image_now.shape, F32),
            jax.ShapeDtypeStruct((1, 1), F32),
        ),
        in_specs=[anywhere, vmem, vmem, anywhere],
        out_specs=(anywhere, vmem),
        scratch_shapes=[
            pltpu.VMEM((10, 2, 2, 256, 128), F32),
            pltpu.VMEM((10, 2, 512, 128), BF16),
            pltpu.VMEM((10, 2, 512, 128), BF16),
            pltpu.VMEM((768, 256), BF16),
            pltpu.VMEM((768, 256), BF16),
            pltpu.VMEM((5, 512, 512), BF16),
            pltpu.VMEM((5, 512, 512), BF16),
            pltpu.VMEM((8, 512, 256), F32),
            pltpu.VMEM((7, 512, 256), F32),
            pltpu.VMEM((512, 256), BF16),
            pltpu.VMEM((512, 256), BF16),
            pltpu.VMEM((8, 512, 256), F32),
            pltpu.VMEM((2, 2, 2064, 128), F32),
            pltpu.VMEM((2, 2, 2048, 128), F32),
            pltpu.VMEM((8, 2048), F32),
            pltpu.VMEM((2, 8, 2048), F32),
            pltpu.VMEM((2 * STAGES + 1, 8, 128), F32),
            dma((9,)), dma((2,)), dma((2,)), dma((7,)), dma((7,)),
            dma((STAGES,)), dma((STAGES,)), dma((2,)), dma((2,)), dma((8,)),
        ],
        compiler_params=pltpu.CompilerParams(
            collective_id=0, has_side_effects=True, vmem_limit_bytes=50 << 20
        ),
        cost_estimate=pl.CostEstimate(
            flops=20_000_000_000, bytes_accessed=12 << 20, transcendentals=0
        ),
        name="sar_step",
    )(residual, range_chirp, az_kernel, image_now)
    return image_next, root_mean.reshape(())


def solution(mesh):
    placed = (
        P(None, None, "az", "rng"),
        P(),
        P(("rng", "az"), None, None),
        P(None, None, None, ("rng", "az")),
    )
    return jax.shard_map(
        local,
        mesh=mesh,
        in_specs=placed,
        out_specs=(P(None, None, None, ("rng", "az")), P()),
        check_vma=False,
    )
```

time: 348 us -> 117 us (0.34)
  blocking collectives: 146 us -> 0 us
  Pallas kernels: 0 us -> 109 us
  local copies, waits for them, and re-layouts: 96.3 us -> 5.84 us
  matrix products: 61.4 us -> 0 us
  other arithmetic: 28.8 us -> 0 us
  starting transfers between devices: 10.4 us -> 0 us
    pallas_call x0 -> x1, Pallas kernels: none -> 109 us  [local(): pl.pallas_call(kernel, out_shape=(jax.ShapeDtypeStruct(image_now.shape, F...]
    psum x1 -> x0, blocking collectives: 86.8 us -> none  [local(): grand_total = lax.psum(own_sum, ('rng', 'az'))]
    dot_general x2 -> x0, matrix products: 61.4 us -> none  [the longest x1 46.5 us: azimuth_correlate(): jnp.einsum('oiqm,pqtmw->potiw', matrix, windows, precision=lax.Precision....]
    all_to_all x1 -> x0, blocking collectives: 59.1 us -> none  [corner_turn(): lax.all_to_all(echo_part, 'az', split_axis=3, concat_axis=2, tiled=True)]
    unnamed x17 -> x5, local copies, waits for them, and re-layouts: 34 us -> 5.84 us
    slice x8 -> x0, local copies, waits for them, and re-layouts: 20.6 us -> none  [the longest x1 8.04 us: padded_2(): head = lax.slice_in_dim(cells, 0, width, axis=dim)]
    another operation x10 -> x0, local copies, waits for them, and re-layouts: 19.9 us -> none  [the longest x8 12.6 us: toeplitz_rows(): flattened = jnp.tile(padded, row_count)[:row_count * col_count]]
    sub x1 -> x0, other arithmetic: 14.7 us -> none  [local(): image_now - step_size * (adjoint / root_mean + reg_weight * laplacian(ima...]
  transfers between devices with their start and end apart: 4 -> 0, of which waited for: 0 -> 0; matrix products, arithmetic and copies ran while one was open for 18% -> 0% of each run, Pallas kernels for 0% -> 0%
where the time goes in v1:
time: 117 us
  Pallas kernels  109 us (93%)
  local copies, waits for them, and re-layouts  5.84 us (5%)
  between operations  2.34 us (2%)
    pallas_call x1, Pallas kernels, local(): pl.pallas_call(kernel, out_shape=(jax.ShapeDtypeStruct(image_now.shape, F...  109 us
    unnamed x5, local copies, waits for them, and re-layouts  5.84 us

profile of v1, /device:TPU:0, one launch (start us, length us, event | category | flops | bytes accessed | tf_op | source)
XLA Modules:
  0.0 117.1 jit_solution(511820914097448762)
XLA Ops:
  0.6 0.0 copy-start
  0.6 0.7 copy-done
  1.3 0.0 copy-start.1
  1.3 0.7 copy-done.1
  2.0 108.9 %sar_step.1 = (f32[2,2,2048,128]{3,2,1,0:T(8,128)}, f32[1,1]{1,0:T(1,128)}) custom-call(f32[2,2,256,1024]{3,2,1,0:T(8,128)} %res.1, f32[2,256]{1,0:T(2,128)S(1)} %copy-done.1, f32[1,2,1024]{2,1,0:T(2,128)S(1)} %copy-done, f32[2,2,2048,128]{3,2,1,0:T(8,128)} %img.1), custom_call_target="tpu_custom_call" | custom-call | flops 20000000000 | bytes 12582912 | tf_op jit(solution)/shard_map/sar_step/pallas_call | solution.py:336
  110.9 4.5 %copy.8 = f32[2,2,2048,128]{3,2,1,0:T(8,128)} copy(f32[2,2,2048,128]{3,2,1,0:T(8,128)} %get-tuple-element.8) | data formatting | bytes 8388608
Async XLA Ops:
  0.6 0.7 copy-start
  1.3 0.7 copy-start.1

commit v2 on v0

v2 whole, which is shorter than its diff:
```python
import jax
import jax.numpy as jnp
from jax import lax
from jax.experimental import pallas as pl
from jax.experimental.pallas import tpu as pltpu
from jax.sharding import PartitionSpec as P

step_size = 0.5
reg_weight = 0.25
epsilon = 1e-06

F32 = jnp.float32
BF16 = jnp.bfloat16
MESH = pl.DeviceIdType.MESH
GROUP = 8
OTHERS = GROUP - 1
COLS = 16
PARTS = 2
UNIT = 128
TURN = ((0, 1), (1, 0), (2, 1), (3, 0), (1, 1), (2, 0), (3, 1))


def dot(a, b):
    return jnp.dot(a, b, preferred_element_type=F32)


def split(value):
    high = value.astype(BF16)
    return high, (value - high.astype(F32)).astype(BF16)


def toeplitz(row, rows):
    wide = jnp.broadcast_to(row, (rows, row.shape[1]))
    return pltpu.roll(wide, 0, 1, stride=1, stride_axis=0)


def kernel(
    res, chirp, azk, img,
    out, rm_out,
    xf, xh, xl, cv, av, ch, cl, az_mat, sb, rv, x3, im, pk, pc, sm,
    ld, hs, hr, ss, rs, ps, pr, qs, qr, cs, cr,
):
    rng, az = lax.axis_index("rng"), lax.axis_index("az")
    zh, y = az // 4, az % 4
    flat = rng * 8 + az
    to_az = [((zh + dz) % 2) * 4 + (y + dy) % 4 for dy, dz in TURN]
    to_rng = [(rng + k) % COLS for k in range(1, COLS)]
    rng_next, rng_prev = (rng + 1) % 16, (rng + 15) % 16
    col_next, col_prev = (flat + 1) % 128, (flat + 127) % 128

    def load_block(b):
        return pltpu.make_async_copy(
            res.at[:, :, :, pl.ds(128 * b, 128)], xf.at[b + 1], ld.at[b]
        )

    load_chirp = pltpu.make_async_copy(chirp, cv, ld.at[8])
    load_azk = pltpu.make_async_copy(azk.at[0], av, ld.at[9])
    load_img = [
        pltpu.make_async_copy(img.at[q // 2, q % 2], im.at[q, pl.ds(8, 2048)], ld.at[10 + q])
        for q in range(4)
    ]
    for b in range(8):
        load_block(b).start()
    load_chirp.start()
    load_azk.start()
    for copy in load_img:
        copy.start()

    barrier = pltpu.get_barrier_semaphore()
    peers = [(rng, target) for target in to_az]
    peers += [(target, az) for target in to_rng]
    peers += [(col_next // 8, col_next % 8), (col_prev // 8, col_prev % 8)]
    for peer in peers:
        pl.semaphore_signal(barrier, inc=1, device_id=peer, device_id_type=MESH)

    for b in range(8):
        load_block(b).wait()

    def squares(b, total):
        for p in range(2):
            for c in range(2):
                v = xf[b, p, c]
                total += jnp.sum((v * v).reshape(32, 8, 128), axis=0)
        return total

    sm[az] = lax.fori_loop(1, 9, squares, jnp.zeros((8, 128), F32))

    pl.semaphore_wait(barrier, len(peers))

    def halo_copy(side, h):
        lines = pl.ds(UNIT * h, UNIT)
        return pltpu.make_async_remote_copy(
            src_ref=res.at[:, :, lines, pl.ds((896, 0)[side], 128)],
            dst_ref=xf.at[(0, 9)[side], :, :, lines],
            send_sem=hs.at[2 * h + side], recv_sem=hr.at[2 * h + side],
            device_id=((rng_next, rng_prev)[side], az), device_id_type=MESH,
        )

    def part_copy(t):
        return pltpu.make_async_remote_copy(
            src_ref=sm.at[az], dst_ref=sm.at[az], send_sem=ps.at[t], recv_sem=pr.at[t],
            device_id=(rng, to_az[t]), device_id_type=MESH,
        )

    for t in range(OTHERS):
        part_copy(t).start()
    for h in range(PARTS):

        @pl.when(rng < 15)
        def _(h=h):
            halo_copy(0, h).start()

        @pl.when(rng > 0)
        def _(h=h):
            halo_copy(1, h).start()

    load_chirp.wait()
    lanes = jnp.zeros((1, 128), F32)
    cr_t = toeplitz(jnp.concatenate([cv[0:1, :], lanes], 1), 128).T
    ci_t = toeplitz(jnp.concatenate([cv[1:2, :], lanes], 1), 128).T
    for rows, left, right in ((0, cr_t, -ci_t), (384, ci_t, cr_t)):
        for cols, part in ((0, left), (128, right)):
            high, low = split(part)
            ch[rows : rows + 384, cols : cols + 128] = high
            cl[rows : rows + 384, cols : cols + 128] = low

    for t in range(OTHERS):
        part_copy(t).wait()
    total = sm[0]
    for k in range(1, GROUP):
        total += sm[k]
    sm[GROUP + rng] = total

    def total_copy(t):
        return pltpu.make_async_remote_copy(
            src_ref=sm.at[GROUP + rng], dst_ref=sm.at[GROUP + rng],
            send_sem=qs.at[t], recv_sem=qr.at[t],
            device_id=(to_rng[t], az), device_id_type=MESH,
        )

    for t in range(COLS - 1):
        total_copy(t).start()

    def split_lines(b, h):
        lines = slice(UNIT * h, UNIT * (h + 1))
        for p in range(2):
            for c in range(2):
                high, low = split(xf[b, p, c, lines])
                xh[b, c, h, p * UNIT : (p + 1) * UNIT] = high
                xl[b, c, h, p * UNIT : (p + 1) * UNIT] = low

    def split_block(b, carry):
        for h in range(PARTS):
            split_lines(b, h)
        return carry

    lax.fori_loop(1, 9, split_block, 0)

    for copy in load_img:
        copy.wait()
    lane = lax.broadcasted_iota(jnp.int32, (8, 128), 1)
    pair = lane // 2
    for q in range(4):
        im[q, 0:8] = jnp.zeros((8, 128), F32)
        im[q, 2056:2064] = jnp.zeros((8, 128), F32)

        def pack(k, carry, q=q):
            at = pl.multiple_of(512 * k, 512) + 8
            packed = jnp.zeros((8, 128), F32)
            for g in range(64):
                turned = pltpu.roll(im[q, pl.ds(at + 8 * g, 8), :], 2 * g + 1, 1)
                packed = jnp.where(pair == g, turned, packed)
            pk[4 * q + k] = packed
            return carry

        lax.fori_loop(0, 4, pack, 0)

    def column_copy(side, target):
        return pltpu.make_async_remote_copy(
            src_ref=pk, dst_ref=pc.at[side], send_sem=cs.at[side], recv_sem=cr.at[side],
            device_id=(target // 8, target % 8), device_id_type=MESH,
        )

    cols = [column_copy(0, col_next), column_copy(1, col_prev)]
    for copy in cols:
        copy.start()

    for t in range(COLS - 1):
        total_copy(t).wait()
    total = sm[GROUP]
    for k in range(1, COLS):
        total += sm[GROUP + k]
    total = jnp.sum(total, axis=(0, 1), keepdims=True)
    root_mean = jnp.sqrt(total / (2.0 * 2048 * 16384) + epsilon)
    rm_out[...] = root_mean

    def range_block(j, h, slot):
        high = jnp.concatenate([xh[j + q, c, h] for c in range(2) for q in range(3)], 1)
        low = jnp.concatenate([xl[j + q, c, h] for c in range(2) for q in range(3)], 1)
        result = dot(high, ch[...]) + dot(low, ch[...]) + dot(high, cl[...])
        for p in range(2):
            for c in range(2):
                sb[slot, c * UNIT : (c + 1) * UNIT, p * 128 : (p + 1) * 128] = result[
                    p * UNIT : (p + 1) * UNIT, c * 128 : (c + 1) * 128
                ]

    def turn_copy(h, t):
        dz, dy = 1 - t % 2, t - 3 * (t // 4)
        target = ((zh + dz) % 2) * 4 + (y + dy) % 4
        source = ((zh + dz) % 2) * 4 + (y + 4 - dy) % 4
        slot = OTHERS * h + t
        return target, source, pltpu.make_async_remote_copy(
            src_ref=sb.at[slot], dst_ref=rv.at[slot], send_sem=ss.at[slot], recv_sem=rs.at[slot],
            device_id=(rng, target), device_id_type=MESH,
        )

    for h in range(PARTS):

        @pl.when(rng > 0)
        def _(h=h):
            halo_copy(0, h).wait_recv()

        @pl.when(rng == 0)
        def _(h=h):
            xf[0, :, :, UNIT * h : UNIT * (h + 1)] = jnp.zeros((2, 2, UNIT, 128), F32)

        @pl.when(rng < 15)
        def _(h=h):
            halo_copy(1, h).wait_recv()

        @pl.when(rng == 15)
        def _(h=h):
            xf[9, :, :, UNIT * h : UNIT * (h + 1)] = jnp.zeros((2, 2, UNIT, 128), F32)

        split_lines(0, h)
        split_lines(9, h)

        def send(t, carry, h=h):
            target, _, copy = turn_copy(h, t)
            range_block(target, h, OTHERS * h + t)
            copy.start()
            return carry

        lax.fori_loop(0, OTHERS, send, 0)

    def own(h, carry):
        range_block(az, h, OTHERS * PARTS + h)
        return carry

    lax.fori_loop(0, PARTS, own, 0)

    load_azk.wait()
    lanes = jnp.zeros((1, UNIT), F32)
    factor = -step_size / root_mean
    wr = toeplitz(jnp.concatenate([av[0:1, :] * factor, lanes], 1), UNIT)
    wi = toeplitz(jnp.concatenate([av[1:2, :] * factor, lanes], 1), UNIT)
    for k in range(9):
        e = UNIT * (8 - k)
        part_r, part_i = wr[:, e : e + UNIT], wi[:, e : e + UNIT]
        for c, left, right in ((0, part_r, part_i), (1, -part_i, part_r)):
            rows = slice((2 * k + c) * UNIT, (2 * k + c + 1) * UNIT)
            for at, part in ((0, left), (UNIT, right)):
                high, low = split(part)
                az_mat[rows, at : at + UNIT] = high
                az_mat[rows, at + 2 * UNIT : at + 3 * UNIT] = high
                az_mat[rows, at + 4 * UNIT : at + 5 * UNIT] = low

    for copy in cols:
        copy.wait_recv()
    has_prev = jnp.where(flat > 0, 1.0, 0.0)
    has_next = jnp.where(flat < 127, 1.0, 0.0)
    wide = lax.broadcasted_iota(jnp.int32, (64, 128), 1)
    for q in range(4):

        def regularize(k, carry, q=q):
            at = pl.multiple_of(512 * k, 512)
            edge = jnp.where(
                lane % 2 == 0,
                pltpu.roll(pc[1, 4 * q + k], 127, 1) * has_next,
                pltpu.roll(pc[0, 4 * q + k], 1, 1) * has_prev,
            )
            for h in range(8):
                sides = jnp.concatenate(
                    [pltpu.roll(edge, 127 - 2 * g, 1) for g in range(8 * h, 8 * h + 8)], 0
                )
                v = im[q, pl.ds(at + 64 * h, 80), :]
                mid = v[8:72]
                left = jnp.where(wide == 0, sides, pltpu.roll(mid, 1, 1))
                right = jnp.where(wide == 127, sides, pltpu.roll(mid, 127, 1))
                lap = 4.0 * mid - v[9:73] - v[7:71] - right - left
                out[q // 2, q % 2, pl.ds(at + 64 * h, 64), :] = (
                    mid - (step_size * reg_weight) * lap
                )
            return carry

        lax.fori_loop(0, 4, regularize, 0)

    def azimuth(source, unit):
        high, low = split(source)
        x3[0 : 2 * UNIT] = high
        x3[2 * UNIT : 4 * UNIT] = low
        x3[4 * UNIT : 6 * UNIT] = high
        part = dot(az_mat[...], x3[...])
        for k in range(9):
            v = unit - 4 + k

            @pl.when(jnp.logical_and(v >= 0, v < 2048 // UNIT))
            def _(k=k, v=v):
                lines = pl.ds(pl.multiple_of(UNIT * v, UNIT), UNIT)
                for p in range(2):
                    for c in range(2):
                        at = (2 * k + c) * UNIT
                        out[p, c, lines, :] += part[at : at + UNIT, p * 128 : (p + 1) * 128]

    def own_azimuth(h, carry):
        azimuth(sb[OTHERS * PARTS + h], PARTS * az + h)
        return carry

    lax.fori_loop(0, PARTS, own_azimuth, 0)

    def turn_azimuth(n, carry):
        h, t = n // OTHERS, n % OTHERS
        _, source, copy = turn_copy(h, t)
        copy.wait_recv()
        azimuth(rv[n], PARTS * source + h)
        return carry

    lax.fori_loop(0, PARTS * OTHERS, turn_azimuth, 0)

    for h in range(PARTS):
        for t in range(OTHERS):
            turn_copy(h, t)[2].wait_send()

        @pl.when(rng < 15)
        def _(h=h):
            halo_copy(0, h).wait_send()

        @pl.when(rng > 0)
        def _(h=h):
            halo_copy(1, h).wait_send()

    for copy in cols:
        copy.wait_send()


def local(residual, range_chirp, az_kernel, image_now):
    vmem = pl.BlockSpec(memory_space=pltpu.VMEM)
    hbm = pl.BlockSpec(memory_space=pltpu.HBM)
    dma = pltpu.SemaphoreType.DMA
    turns = PARTS * OTHERS
    image_next, root_mean = pl.pallas_call(
        kernel,
        out_shape=(
            pltpu.VMEM(image_now.shape, F32),
            jax.ShapeDtypeStruct((1, 1), F32),
        ),
        in_specs=[hbm] * 4,
        out_specs=(vmem, vmem),
        scratch_shapes=[
            pltpu.VMEM((10, 2, 2, 256, 128), F32),
            pltpu.VMEM((10, 2, PARTS, 2 * UNIT, 128), BF16),
            pltpu.VMEM((10, 2, PARTS, 2 * UNIT, 128), BF16),
            pltpu.VMEM((2, 256), F32),
            pltpu.VMEM((2, 1024), F32),
            pltpu.VMEM((768, 256), BF16),
            pltpu.VMEM((768, 256), BF16),
            pltpu.VMEM((18 * UNIT, 6 * UNIT), BF16),
            pltpu.VMEM((turns + PARTS, 2 * UNIT, 256), F32),
            pltpu.VMEM((turns, 2 * UNIT, 256), F32),
            pltpu.VMEM((6 * UNIT, 256), BF16),
            pltpu.VMEM((4, 2064, 128), F32),
            pltpu.VMEM((16, 8, 128), F32),
            pltpu.VMEM((2, 16, 8, 128), F32),
            pltpu.VMEM((GROUP + COLS, 8, 128), F32),
            dma((14,)), dma((2 * PARTS,)), dma((2 * PARTS,)), dma((turns,)), dma((turns,)),
            dma((OTHERS,)), dma((OTHERS,)), dma((COLS - 1,)), dma((COLS - 1,)),
            dma((2,)), dma((2,)),
        ],
        compiler_params=pltpu.CompilerParams(
            collective_id=0, has_side_effects=True, vmem_limit_bytes=50 << 20
        ),
        cost_estimate=pl.CostEstimate(
            flops=20_000_000_000, bytes_accessed=12 << 20, transcendentals=0
        ),
        name="sar_step",
    )(residual, range_chirp, az_kernel, image_now)
    return image_next, root_mean.reshape(())


def solution(mesh):
    placed = (
        P(None, None, "az", "rng"),
        P(),
        P(("rng", "az"), None, None),
        P(None, None, None, ("rng", "az")),
    )
    return jax.shard_map(
        local,
        mesh=mesh,
        in_specs=placed,
        out_specs=(P(None, None, None, ("rng", "az")), P()),
        check_vma=False,
    )
```

time: 348 us -> 75 us (0.22)
  blocking collectives: 146 us -> 0 us
  local copies, waits for them, and re-layouts: 96.3 us -> 2.02 us
  Pallas kernels: 0 us -> 70.1 us
  matrix products: 61.4 us -> 0 us
  other arithmetic: 28.8 us -> 0 us
  starting transfers between devices: 10.4 us -> 0 us
    psum x1 -> x0, blocking collectives: 86.8 us -> none  [local(): grand_total = lax.psum(own_sum, ('rng', 'az'))]
    pallas_call x0 -> x1, Pallas kernels: none -> 70.1 us  [local(): pl.pallas_call(kernel, out_shape=(pltpu.VMEM(image_now.shape, F32), jax.S...]
    dot_general x2 -> x0, matrix products: 61.4 us -> none  [the longest x1 46.5 us: azimuth_correlate(): jnp.einsum('oiqm,pqtmw->potiw', matrix, windows, precision=lax.Precision....]
    all_to_all x1 -> x0, blocking collectives: 59.1 us -> none  [corner_turn(): lax.all_to_all(echo_part, 'az', split_axis=3, concat_axis=2, tiled=True)]
    unnamed x17 -> x1, local copies, waits for them, and re-layouts: 34 us -> 2.02 us
    slice x8 -> x0, local copies, waits for them, and re-layouts: 20.6 us -> none  [the longest x1 8.04 us: padded_2(): head = lax.slice_in_dim(cells, 0, width, axis=dim)]
    another operation x10 -> x0, local copies, waits for them, and re-layouts: 19.9 us -> none  [the longest x8 12.6 us: toeplitz_rows(): flattened = jnp.tile(padded, row_count)[:row_count * col_count]]
    sub x1 -> x0, other arithmetic: 14.7 us -> none  [local(): image_now - step_size * (adjoint / root_mean + reg_weight * laplacian(ima...]
  transfers between devices with their start and end apart: 4 -> 0, of which waited for: 0 -> 0; matrix products, arithmetic and copies ran while one was open for 18% -> 0% of each run, Pallas kernels for 0% -> 0%
where the time goes in v2:
time: 75 us; the launch traced here: 74.4 us
  Pallas kernels  70.1 us (93%)
  between operations  2.33 us (3%)
  local copies, waits for them, and re-layouts  2.02 us (3%)
    pallas_call x1, Pallas kernels, local(): pl.pallas_call(kernel, out_shape=(pltpu.VMEM(image_now.shape, F32), jax.S...  70.1 us
    unnamed x1, local copies, waits for them, and re-layouts  2.02 us

profile of v2, /device:TPU:0, one launch (start us, length us, event | category | flops | bytes accessed | tf_op | source)
XLA Modules:
  0.0 74.4 jit_solution(7776165936721793722)
XLA Ops:
  0.6 70.1 %sar_step.1 = (f32[2,2,2048,128]{3,2,1,0:T(8,128)S(1)}, f32[1,1]{1,0:T(1,128)}) custom-call(f32[2,2,256,1024]{3,2,1,0:T(8,128)} %res.1, f32[2,256]{1,0:T(2,128)} %chirp.1, f32[1,2,1024]{2,1,0:T(2,128)} %azk.1, f32[2,2,2048,128]{3,2,1,0:T(8,128)} %img.1), custom_call_target="tpu_custom_call" | custom-call | flops 20000000000 | bytes 12582912 | tf_op jit(solution)/shard_map/sar_step/pallas_call | solution.py:351
  70.7 2.0 %copy.8 = f32[2,2,2048,128]{3,2,1,0:T(8,128)} copy(f32[2,2,2048,128]{3,2,1,0:T(8,128)S(1)} %get-tuple-element.6) | data formatting | bytes 8388608

commit v3 on v2

--- a/solution.py
+++ b/solution.py
@@ -16,6 +16,7 @@
 OTHERS = GROUP - 1
 COLS = 16
 PARTS = 2
+LATE = 4
 UNIT = 128
 TURN = ((0, 1), (1, 0), (2, 1), (3, 0), (1, 1), (2, 0), (3, 1))
 
@@ -38,7 +39,7 @@
     res, chirp, azk, img,
     out, rm_out,
     xf, xh, xl, cv, av, ch, cl, az_mat, sb, rv, x3, im, pk, pc, sm,
-    ld, hs, hr, ss, rs, ps, pr, qs, qr, cs, cr,
+    ld, hs, hr, ss, rs, ps, pr, qs, qr, cs, cr, go, ready,
 ):
     rng, az = lax.axis_index("rng"), lax.axis_index("az")
     zh, y = az // 4, az % 4
@@ -59,9 +60,9 @@
         pltpu.make_async_copy(img.at[q // 2, q % 2], im.at[q, pl.ds(8, 2048)], ld.at[10 + q])
         for q in range(4)
     ]
+    load_chirp.start()
     for b in range(8):
         load_block(b).start()
-    load_chirp.start()
     load_azk.start()
     for copy in load_img:
         copy.start()
@@ -72,47 +73,6 @@
     peers += [(col_next // 8, col_next % 8), (col_prev // 8, col_prev % 8)]
     for peer in peers:
         pl.semaphore_signal(barrier, inc=1, device_id=peer, device_id_type=MESH)
-
-    for b in range(8):
-        load_block(b).wait()
-
-    def squares(b, total):
-        for p in range(2):
-            for c in range(2):
-                v = xf[b, p, c]
-                total += jnp.sum((v * v).reshape(32, 8, 128), axis=0)
-        return total
-
-    sm[az] = lax.fori_loop(1, 9, squares, jnp.zeros((8, 128), F32))
-
-    pl.semaphore_wait(barrier, len(peers))
-
-    def halo_copy(side, h):
-        lines = pl.ds(UNIT * h, UNIT)
-        return pltpu.make_async_remote_copy(
-            src_ref=res.at[:, :, lines, pl.ds((896, 0)[side], 128)],
-            dst_ref=xf.at[(0, 9)[side], :, :, lines],
-            send_sem=hs.at[2 * h + side], recv_sem=hr.at[2 * h + side],
-            device_id=((rng_next, rng_prev)[side], az), device_id_type=MESH,
-        )
-
-    def part_copy(t):
-        return pltpu.make_async_remote_copy(
-            src_ref=sm.at[az], dst_ref=sm.at[az], send_sem=ps.at[t], recv_sem=pr.at[t],
-            device_id=(rng, to_az[t]), device_id_type=MESH,
-        )
-
-    for t in range(OTHERS):
-        part_copy(t).start()
-    for h in range(PARTS):
-
-        @pl.when(rng < 15)
-        def _(h=h):
-            halo_copy(0, h).start()
-
-        @pl.when(rng > 0)
-        def _(h=h):
-            halo_copy(1, h).start()
 
     load_chirp.wait()
     lanes = jnp.zeros((1, 128), F32)
@@ -124,22 +84,46 @@
             ch[rows : rows + 384, cols : cols + 128] = high
             cl[rows : rows + 384, cols : cols + 128] = low
 
+    for b in range(8):
+        load_block(b).wait()
+
+    def squares(b, total):
+        for p in range(2):
+            for c in range(2):
+                v = xf[b, p, c]
+                total += jnp.sum((v * v).reshape(32, 8, 128), axis=0)
+        return total
+
+    sm[az] = lax.fori_loop(1, 9, squares, jnp.zeros((8, 128), F32))
+
+    pl.semaphore_wait(barrier, len(peers))
+
+    def halo_copy(side, h):
+        lines = pl.ds(UNIT * h, UNIT)
+        return pltpu.make_async_remote_copy(
+            src_ref=res.at[:, :, lines, pl.ds((896, 0)[side], 128)],
+            dst_ref=xf.at[(0, 9)[side], :, :, lines],
+            send_sem=hs.at[2 * h + side], recv_sem=hr.at[2 * h + side],
+            device_id=((rng_next, rng_prev)[side], az), device_id_type=MESH,
+        )
+
+    def part_copy(t):
+        return pltpu.make_async_remote_copy(
+            src_ref=sm.at[az], dst_ref=sm.at[az], send_sem=ps.at[t], recv_sem=pr.at[t],
+            device_id=(rng, to_az[t]), device_id_type=MESH,
+        )
+
     for t in range(OTHERS):
-        part_copy(t).wait()
-    total = sm[0]
-    for k in range(1, GROUP):
-        total += sm[k]
-    sm[GROUP + rng] = total
-
-    def total_copy(t):
-        return pltpu.make_async_remote_copy(
-            src_ref=sm.at[GROUP + rng], dst_ref=sm.at[GROUP + rng],
-            send_sem=qs.at[t], recv_sem=qr.at[t],
-            device_id=(to_rng[t], az), device_id_type=MESH,
-        )
-
-    for t in range(COLS - 1):
-        total_copy(t).start()
+        part_copy(t).start()
+    for h in range(PARTS):
+
+        @pl.when(rng < 15)
+        def _(h=h):
+            halo_copy(0, h).start()
+
+        @pl.when(rng > 0)
+        def _(h=h):
+            halo_copy(1, h).start()
 
     def split_lines(b, h):
         lines = slice(UNIT * h, UNIT * (h + 1))
@@ -149,50 +133,31 @@
                 xh[b, c, h, p * UNIT : (p + 1) * UNIT] = high
                 xl[b, c, h, p * UNIT : (p + 1) * UNIT] = low
 
-    def split_block(b, carry):
-        for h in range(PARTS):
+    def split_part(h):
+        def body(b, carry):
             split_lines(b, h)
-        return carry
-
-    lax.fori_loop(1, 9, split_block, 0)
-
-    for copy in load_img:
-        copy.wait()
-    lane = lax.broadcasted_iota(jnp.int32, (8, 128), 1)
-    pair = lane // 2
-    for q in range(4):
-        im[q, 0:8] = jnp.zeros((8, 128), F32)
-        im[q, 2056:2064] = jnp.zeros((8, 128), F32)
-
-        def pack(k, carry, q=q):
-            at = pl.multiple_of(512 * k, 512) + 8
-            packed = jnp.zeros((8, 128), F32)
-            for g in range(64):
-                turned = pltpu.roll(im[q, pl.ds(at + 8 * g, 8), :], 2 * g + 1, 1)
-                packed = jnp.where(pair == g, turned, packed)
-            pk[4 * q + k] = packed
             return carry
 
-        lax.fori_loop(0, 4, pack, 0)
-
-    def column_copy(side, target):
+        lax.fori_loop(1, 9, body, 0)
+
+    split_part(0)
+
+    for t in range(OTHERS):
+        part_copy(t).wait()
+    total = sm[0]
+    for k in range(1, GROUP):
+        total += sm[k]
+    sm[GROUP + rng] = total
+
+    def total_copy(t):
         return pltpu.make_async_remote_copy(
-            src_ref=pk, dst_ref=pc.at[side], send_sem=cs.at[side], recv_sem=cr.at[side],
-            device_id=(target // 8, target % 8), device_id_type=MESH,
-        )
-
-    cols = [column_copy(0, col_next), column_copy(1, col_prev)]
-    for copy in cols:
-        copy.start()
+            src_ref=sm.at[GROUP + rng], dst_ref=sm.at[GROUP + rng],
+            send_sem=qs.at[t], recv_sem=qr.at[t],
+            device_id=(to_rng[t], az), device_id_type=MESH,
+        )
 
     for t in range(COLS - 1):
-        total_copy(t).wait()
-    total = sm[GROUP]
-    for k in range(1, COLS):
-        total += sm[GROUP + k]
-    total = jnp.sum(total, axis=(0, 1), keepdims=True)
-    root_mean = jnp.sqrt(total / (2.0 * 2048 * 16384) + epsilon)
-    rm_out[...] = root_mean
+        total_copy(t).start()
 
     def range_block(j, h, slot):
         high = jnp.concatenate([xh[j + q, c, h] for c in range(2) for q in range(3)], 1)
@@ -214,28 +179,43 @@
             device_id=(rng, target), device_id_type=MESH,
         )
 
-    for h in range(PARTS):
+    def send_part(h):
 
         @pl.when(rng > 0)
-        def _(h=h):
+        def _():
             halo_copy(0, h).wait_recv()
 
         @pl.when(rng == 0)
-        def _(h=h):
+        def _():
             xf[0, :, :, UNIT * h : UNIT * (h + 1)] = jnp.zeros((2, 2, UNIT, 128), F32)
 
         @pl.when(rng < 15)
-        def _(h=h):
+        def _():
             halo_copy(1, h).wait_recv()
 
         @pl.when(rng == 15)
-        def _(h=h):
+        def _():
             xf[9, :, :, UNIT * h : UNIT * (h + 1)] = jnp.zeros((2, 2, UNIT, 128), F32)
 
+        if h == 0:
+            for near, end in ((1, 0), (COLS - 2, COLS - 1)):
+
+                @pl.when(rng == near)
+                def _():
+                    pl.semaphore_signal(go, inc=1, device_id=(end, az), device_id_type=MESH)
+
+                @pl.when(rng == end)
+                def _():
+                    pl.semaphore_wait(go, 1)
+
+        if h == 0:
+            for target in to_az:
+                pl.semaphore_signal(ready, inc=1, device_id=(rng, target), device_id_type=MESH)
+            pl.semaphore_wait(ready, OTHERS)
         split_lines(0, h)
         split_lines(9, h)
 
-        def send(t, carry, h=h):
+        def send(t, carry):
             target, _, copy = turn_copy(h, t)
             range_block(target, h, OTHERS * h + t)
             copy.start()
@@ -243,11 +223,55 @@
 
         lax.fori_loop(0, OTHERS, send, 0)
 
+    send_part(0)
+
+    for copy in load_img:
+        copy.wait()
+    lane = lax.broadcasted_iota(jnp.int32, (8, 128), 1)
+    for q in range(4):
+        im[q, 0:8] = jnp.zeros((8, 128), F32)
+        im[q, 2056:2064] = jnp.zeros((8, 128), F32)
+
+        def pack(k, carry, q=q):
+            at = pl.multiple_of(1024 * k, 1024) + 8
+            head = tail = jnp.zeros((8, 128), F32)
+            for g in range(128):
+                turned = pltpu.roll(im[q, pl.ds(at + 8 * g, 8), :], g, 1)
+                head = jnp.where(lane == g, turned, head)
+                tail = jnp.where(lane == (g + 127) % 128, turned, tail)
+            pk[0, 2 * q + k] = tail
+            pk[1, 2 * q + k] = head
+            return carry
+
+        lax.fori_loop(0, 2, pack, 0)
+
+    def column_copy(side, target):
+        return pltpu.make_async_remote_copy(
+            src_ref=pk.at[side], dst_ref=pc.at[side], send_sem=cs.at[side], recv_sem=cr.at[side],
+            device_id=(target // 8, target % 8), device_id_type=MESH,
+        )
+
+    cols = [column_copy(0, col_next), column_copy(1, col_prev)]
+    for copy in cols:
+        copy.start()
+
+    split_part(1)
+    send_part(1)
+
     def own(h, carry):
         range_block(az, h, OTHERS * PARTS + h)
         return carry
 
     lax.fori_loop(0, PARTS, own, 0)
+
+    for t in range(COLS - 1):
+        total_copy(t).wait()
+    total = sm[GROUP]
+    for k in range(1, COLS):
+        total += sm[GROUP + k]
+    total = jnp.sum(total, axis=(0, 1), keepdims=True)
+    root_mean = jnp.sqrt(total / (2.0 * 2048 * 16384) + epsilon)
+    rm_out[...] = root_mean
 
     load_azk.wait()
     lanes = jnp.zeros((1, UNIT), F32)
@@ -265,36 +289,6 @@
                 az_mat[rows, at + 2 * UNIT : at + 3 * UNIT] = high
                 az_mat[rows, at + 4 * UNIT : at + 5 * UNIT] = low
 
-    for copy in cols:
-        copy.wait_recv()
-    has_prev = jnp.where(flat > 0, 1.0, 0.0)
-    has_next = jnp.where(flat < 127, 1.0, 0.0)
-    wide = lax.broadcasted_iota(jnp.int32, (64, 128), 1)
-    for q in range(4):
-
-        def regularize(k, carry, q=q):
-            at = pl.multiple_of(512 * k, 512)
-            edge = jnp.where(
-                lane % 2 == 0,
-                pltpu.roll(pc[1, 4 * q + k], 127, 1) * has_next,
-                pltpu.roll(pc[0, 4 * q + k], 1, 1) * has_prev,
-            )
-            for h in range(8):
-                sides = jnp.concatenate(
-                    [pltpu.roll(edge, 127 - 2 * g, 1) for g in range(8 * h, 8 * h + 8)], 0
-                )
-                v = im[q, pl.ds(at + 64 * h, 80), :]
-                mid = v[8:72]
-                left = jnp.where(wide == 0, sides, pltpu.roll(mid, 1, 1))
-                right = jnp.where(wide == 127, sides, pltpu.roll(mid, 127, 1))
-                lap = 4.0 * mid - v[9:73] - v[7:71] - right - left
-                out[q // 2, q % 2, pl.ds(at + 64 * h, 64), :] = (
-                    mid - (step_size * reg_weight) * lap
-                )
-            return carry
-
-        lax.fori_loop(0, 4, regularize, 0)
-
     def azimuth(source, unit):
         high, low = split(source)
         x3[0 : 2 * UNIT] = high
@@ -312,6 +306,8 @@
                         at = (2 * k + c) * UNIT
                         out[p, c, lines, :] += part[at : at + UNIT, p * 128 : (p + 1) * 128]
 
+    out[...] = jnp.zeros_like(out)
+
     def own_azimuth(h, carry):
         azimuth(sb[OTHERS * PARTS + h], PARTS * az + h)
         return carry
@@ -325,7 +321,38 @@
         azimuth(rv[n], PARTS * source + h)
         return carry
 
-    lax.fori_loop(0, PARTS * OTHERS, turn_azimuth, 0)
+    lax.fori_loop(0, LATE, turn_azimuth, 0)
+
+    for copy in cols:
+        copy.wait_recv()
+    has_prev = jnp.where(flat > 0, 1.0, 0.0)
+    has_next = jnp.where(flat < 127, 1.0, 0.0)
+    wide = lax.broadcasted_iota(jnp.int32, (64, 128), 1)
+    for q in range(4):
+
+        def regularize(k, carry, q=q):
+            at = pl.multiple_of(512 * k, 512)
+            before = pc[0, 2 * q + k // 2] * has_prev
+            after = pc[1, 2 * q + k // 2] * has_next
+            before = jnp.where(k % 2 == 1, pltpu.roll(before, 64, 1), before)
+            after = jnp.where(k % 2 == 1, pltpu.roll(after, 64, 1), after)
+            for h in range(8):
+                rows = range(8 * h, 8 * h + 8)
+                lefts = jnp.concatenate([pltpu.roll(before, (129 - g) % 128, 1) for g in rows], 0)
+                rights = jnp.concatenate([pltpu.roll(after, 127 - g, 1) for g in rows], 0)
+                v = im[q, pl.ds(at + 64 * h, 80), :]
+                mid = v[8:72]
+                left = jnp.where(wide == 0, lefts, pltpu.roll(mid, 1, 1))
+                right = jnp.where(wide == 127, rights, pltpu.roll(mid, 127, 1))
+                lap = 4.0 * mid - v[9:73] - v[7:71] - right - left
+                out[q // 2, q % 2, pl.ds(at + 64 * h, 64), :] += (
+                    mid - (step_size * reg_weight) * lap
+                )
+            return carry
+
+        lax.fori_loop(0, 4, regularize, 0)
+
+    lax.fori_loop(LATE, PARTS * OTHERS, turn_azimuth, 0)
 
     for h in range(PARTS):
         for t in range(OTHERS):
@@ -369,12 +396,12 @@
             pltpu.VMEM((turns, 2 * UNIT, 256), F32),
             pltpu.VMEM((6 * UNIT, 256), BF16),
             pltpu.VMEM((4, 2064, 128), F32),
-            pltpu.VMEM((16, 8, 128), F32),
-            pltpu.VMEM((2, 16, 8, 128), F32),
+            pltpu.VMEM((2, 8, 8, 128), F32),
+            pltpu.VMEM((2, 8, 8, 128), F32),
             pltpu.VMEM((GROUP + COLS, 8, 128), F32),
             dma((14,)), dma((2 * PARTS,)), dma((2 * PARTS,)), dma((turns,)), dma((turns,)),
             dma((OTHERS,)), dma((OTHERS,)), dma((COLS - 1,)), dma((COLS - 1,)),
-            dma((2,)), dma((2,)),
+            dma((2,)), dma((2,)), pltpu.SemaphoreType.REGULAR, pltpu.SemaphoreType.REGULAR,
         ],
         compiler_params=pltpu.CompilerParams(
             collective_id=0, has_side_effects=True, vmem_limit_bytes=50 << 20

time: 75 us -> 73.7 us (0.983)
  Pallas kernels: 70.1 us -> 69.3 us
    pallas_call x1, Pallas kernels: 70.1 us -> 69.3 us  [local(): pl.pallas_call(kernel, out_shape=(pltpu.VMEM(image_now.shape, F32), jax.S...]
where the time goes in v3:
time: 73.7 us; the launch traced here: 73.6 us
  Pallas kernels  69.3 us (94%)
  between operations  2.33 us (3%)
  local copies, waits for them, and re-layouts  2.02 us (3%)
    pallas_call x1, Pallas kernels, local(): pl.pallas_call(kernel, out_shape=(pltpu.VMEM(image_now.shape, F32), jax.S...  69.3 us
    unnamed x1, local copies, waits for them, and re-layouts  2.02 us

profile of v3, /device:TPU:0, one launch (start us, length us, event | category | flops | bytes accessed | tf_op | source)
XLA Modules:
  0.0 73.6 jit_solution(15598826611756692236)
XLA Ops:
  0.6 69.3 %sar_step.1 = (f32[2,2,2048,128]{3,2,1,0:T(8,128)S(1)}, f32[1,1]{1,0:T(1,128)}) custom-call(f32[2,2,256,1024]{3,2,1,0:T(8,128)} %res.1, f32[2,256]{1,0:T(2,128)} %chirp.1, f32[1,2,1024]{2,1,0:T(2,128)} %azk.1, f32[2,2,2048,128]{3,2,1,0:T(8,128)} %img.1), custom_call_target="tpu_custom_call" | custom-call | flops 20000000000 | bytes 12582912 | tf_op jit(solution)/shard_map/sar_step/pallas_call | solution.py:378
  69.9 2.0 %copy.8 = f32[2,2,2048,128]{3,2,1,0:T(8,128)} copy(f32[2,2,2048,128]{3,2,1,0:T(8,128)S(1)} %get-tuple-element.6) | data formatting | bytes 8388608

commit v4 on v3

--- a/solution.py
+++ b/solution.py
@@ -16,7 +16,7 @@
 OTHERS = GROUP - 1
 COLS = 16
 PARTS = 2
-LATE = 4
+LATE = 2
 UNIT = 128
 TURN = ((0, 1), (1, 0), (2, 1), (3, 0), (1, 1), (2, 0), (3, 1))
 

time: 73.7 us -> 74.2 us (level)
  no operation moved by 1% of the time
where the time goes in v4:
time: 74.2 us; the launch traced here: 73.6 us
  Pallas kernels  69.3 us (93%)
  between operations  2.33 us (3%)
  local copies, waits for them, and re-layouts  2.02 us (3%)
    pallas_call x1, Pallas kernels, local(): pl.pallas_call(kernel, out_shape=(pltpu.VMEM(image_now.shape, F32), jax.S...  69.3 us
    unnamed x1, local copies, waits for them, and re-layouts  2.02 us

profile of v4, /device:TPU:0, one launch (start us, length us, event | category | flops | bytes accessed | tf_op | source)
XLA Modules:
  0.0 73.6 jit_solution(10798026284722941264)
XLA Ops:
  0.6 69.3 %sar_step.1 = (f32[2,2,2048,128]{3,2,1,0:T(8,128)S(1)}, f32[1,1]{1,0:T(1,128)}) custom-call(f32[2,2,256,1024]{3,2,1,0:T(8,128)} %res.1, f32[2,256]{1,0:T(2,128)} %chirp.1, f32[1,2,1024]{2,1,0:T(2,128)} %azk.1, f32[2,2,2048,128]{3,2,1,0:T(8,128)} %img.1), custom_call_target="tpu_custom_call" | custom-call | flops 20000000000 | bytes 12582912 | tf_op jit(solution)/shard_map/sar_step/pallas_call | solution.py:378
  69.9 2.0 %copy.8 = f32[2,2,2048,128]{3,2,1,0:T(8,128)} copy(f32[2,2,2048,128]{3,2,1,0:T(8,128)S(1)} %get-tuple-element.6) | data formatting | bytes 8388608
